TPU v7x, 128 devices: a whole 4x4x4 slice. The times are simulated.
128 devices in a mesh: dp: 8 (over y, core), expert: 16 (over z, x).
Axes of the slice: x: 4, y: 4, z: 4, core: 2. Of those that a mesh axis runs over, the one named last changes fastest.
Arguments:
- patches: bfloat16 [65536, 768], P(('dp', 'expert')), may hold values from -6 to 6
- owner_slot: int32 [512], P(('dp', 'expert')), may hold values from 0 to 511, as said below
- segment_ids: int32 [65536], P(('dp', 'expert')), may hold values from 0 to 511, as said below
- block_mask: int32 [512, 4], P(('dp', 'expert')), may hold values from 0 to 1, as said below
- project_in: bfloat16 [768, 2304], replicated, may hold values from -30 to 30
- project_out: bfloat16 [768, 768], replicated, may hold values from -0.21875 to 0.21875
- slot_keys: bfloat16 [768, 128], replicated, may hold values from -30 to 30
- expert_in: bfloat16 [128, 768, 3072], P(('dp', 'expert')), may hold values from -0.21875 to 0.21875
- expert_out: bfloat16 [128, 3072, 768], P(('dp', 'expert')), may hold values from -0.109375 to 0.109375
Outputs:
- layer_out: bfloat16 [65536, 768], P(('dp', 'expert'))
Inputs may be any that keep to these rules, and one draw needn't show every extreme that they name: A permutation of the 512 blocks. Devices are numbered over dp then expert, and block g is read by device g // 4; it goes to device owner_slot[g] // 4, which has the same index along expert. Each reading device sends exactly 1 block to each of 4 distinct devices along dp, and each device receives exactly 4 blocks. `segment_ids`: Non-decreasing; the rows of run o (rows o * 512 to o * 512 + 511) carry the image numbers o * 4 to o * 4 + 3, each on one row or more. block_mask[o * 4 + a, b] is 1 when blocks a and b of run o hold rows of a common image, else 0.
All inputs are finite; a program needn't handle non-finite values.
Results may differ from a plain program's by a relative error of at most 0.0095.
The roundings to bfloat16 on the way count: a program that leaves them out, or rounds other values in their place, can miss the bound.
Values may be sent and summed in bfloat16 or wider, within the bound.
A program may use at most 128 MiB of HBM per device.

v0:
```python
import jax
import jax.numpy as jnp
from jax import lax
from jax.experimental import pallas as pl
from jax.experimental.pallas import tpu as pltpu
from jax.sharding import PartitionSpec as P

HEADS = 12
HEAD = 64
WIDTH = 768
HALF = WIDTH // 2
HIDDEN = 3072
ROWS = 512
BLOCK = 128
BLOCKS = 4
DP = 8
PEERS = 128
EPS = 1e-06
NEGATIVE = -1e30
GROUPS = 2
GROUP_PEERS = PEERS // GROUPS
CHUNK = 32
MESH = pl.DeviceIdType.MESH
F32 = jnp.float32
BF16 = jnp.bfloat16


def matmul(left, right):
    return jnp.dot(left, right, preferred_element_type=F32)


def matmul_nt(left, right):
    return lax.dot_general(
        left, right, (((1,), (1,)), ((), ())), preferred_element_type=F32
    )


def layer_norm(values):
    centred = values - jnp.mean(values, axis=-1, keepdims=True)
    variance = jnp.mean(centred * centred, axis=-1, keepdims=True)
    return centred * lax.rsqrt(variance + EPS)


def gelu(values):
    return 0.5 * values * (1.0 + lax.erf(values * 0.7071067811865476))


def iota(shape, dim):
    return lax.broadcasted_iota(jnp.int32, shape, dim)


def one_hot(condition):
    return jnp.where(condition, 1.0, 0.0).astype(BF16)


def kernel(
    patches_hbm, owner_ref, segment_ref, mask_ref, in_hbm, out_hbm, keys_hbm, up_hbm, down_hbm,
    result_ref,
    patches, w_in, w_out, w_keys, w_up, w_down,
    stage, slots, place_out, place_in,
    seg_col, image_col, bias, ordered, normed, joint, values_ones, context, hidden, moe_normed,
    slot_send, slot_recv, back_send, back_recv, rows_in, rows_out, mix_weights,
    load_sem, block_send_sem, block_recv_sem, place_send_sem, place_recv_sem,
    slot_send_sem, slot_recv_sem, back_send_sem, back_recv_sem,
):
    dp, ex = lax.axis_index("dp"), lax.axis_index("expert")
    y, core = lax.div(dp, 2), lax.rem(dp, 2)
    z, x = lax.div(ex, 4), lax.rem(ex, 4)

    def ahead(k):
        ax = lax.rem(k, 4)
        az = lax.rem(lax.div(k, 4) + ax, 4)
        ay = lax.rem(lax.div(k, 16) + ax, 4)
        return ax, ay, az, lax.div(k, 64)

    def peer(k, sign):
        ax, ay, az, ac = ahead(k)
        to_y, to_c = lax.rem(y + sign * ay + 4, 4), lax.rem(core + ac, 2)
        to_z, to_x = lax.rem(z + sign * az + 4, 4), lax.rem(x + sign * ax + 4, 4)
        return (to_y * 2 + to_c, to_z * 4 + to_x)

    barrier = pltpu.get_barrier_semaphore()

    def greet(k, carry):
        pl.semaphore_signal(barrier, inc=1, device_id=peer(k, 1), device_id_type=MESH)
        return carry

    lax.fori_loop(1, PEERS, greet, 0)

    loads = [
        pltpu.make_async_copy(source, target, load_sem.at[i])
        for i, (source, target) in enumerate(
            (
                (patches_hbm, patches),
                (in_hbm, w_in),
                (keys_hbm, w_keys),
                (out_hbm, w_out),
                (up_hbm.at[0], w_up),
                (down_hbm.at[0], w_down),
            )
        )
    ]
    for load in loads:
        load.start()

    targets = [lax.div(owner_ref[b], BLOCKS * PEERS // DP) for b in range(BLOCKS)]
    places = [lax.rem(owner_ref[b], BLOCKS) for b in range(BLOCKS)]

    def dp_peer(a, sign):
        return lax.rem(y + sign * (a % 4) + 4, 4) * 2 + lax.rem(core + a // 4, 2)

    loads[0].wait()
    for a in range(DP):
        to = dp_peer(a, 1)
        index, place = jnp.int32(0), jnp.int32(-1)
        for b in range(BLOCKS):
            hit = targets[b] == to
            index = jnp.where(hit, b, index)
            place = jnp.where(hit, places[b], place)
        if a:
            stage[a] = patches[index]
            place_out[a] = jnp.full((8, 128), place, jnp.int32)
        else:
            slots[0] = patches[index]
            place_in[0] = jnp.full((8, 128), place, jnp.int32)

    pl.semaphore_wait(barrier, PEERS - 1)
    sends = []
    for a in (2, 6, 1, 3, 5, 7, 4):
        to = (dp_peer(a, 1), ex)
        for source, target, send, recv in (
            (place_out, place_in, place_send_sem, place_recv_sem),
            (stage, slots, block_send_sem, block_recv_sem),
        ):
            copy = pltpu.make_async_remote_copy(
                src_ref=source.at[a], dst_ref=target.at[a], send_sem=send.at[a], recv_sem=recv.at[a],
                device_id=to, device_id_type=MESH,
            )
            copy.start()
            sends.append(copy)

    segment = segment_ref[...]
    seg_col[...] = jnp.transpose(jnp.broadcast_to(segment.astype(F32), (BLOCK, ROWS)))
    image_col[...] = jnp.transpose(
        jnp.broadcast_to((segment & (BLOCKS - 1)).astype(F32), (BLOCK, ROWS))
    )
    for a in range(BLOCKS):
        for b in range(BLOCKS):
            link = jnp.where(mask_ref[a, b] == 1, 0.0, NEGATIVE)
            rows, columns = slice(a * BLOCK, (a + 1) * BLOCK), slice(b * BLOCK, (b + 1) * BLOCK)
            same = seg_col[rows, :] == segment[:, columns].astype(F32)
            bias[rows, columns] = jnp.where(same, link, NEGATIVE)
    values_ones[:, BLOCK:] = jnp.ones((ROWS, BLOCK), BF16)

    k_lane = iota((PEERS, PEERS), 1)
    ax = k_lane & 3
    az = ((k_lane >> 2) + ax) & 3
    ay = ((k_lane >> 4) + ax) & 3
    ac = k_lane >> 6
    expert_at = ((((y + ay) & 3) * 2 + ((core + ac) & 1)) * 4 + ((z + az) & 3)) * 4 + ((x + ax) & 3)
    reorder = one_hot(iota((PEERS, PEERS), 0) == expert_at)
    for load in loads[1:3]:
        load.wait()
    keys = matmul(w_keys[...], reorder).astype(BF16)

    for copy in sends:
        copy.wait()
    for p in range(BLOCKS):
        where_from = jnp.zeros((8, 128), jnp.int32)
        for a in range(1, DP):
            where_from = jnp.where(place_in[a] == p, a, where_from)
        index = jnp.max(where_from)
        block = slots[index]
        rows = slice(p * BLOCK, (p + 1) * BLOCK)
        ordered[rows, :] = block
        normed[rows, :] = layer_norm(block.astype(F32)).astype(BF16)
    joint[...] = matmul(normed[...], w_in[...]).astype(BF16)

    lane = iota((BLOCK, BLOCK), 1)
    first = lane < HEAD

    def head_pair(i, carry):
        columns = pl.ds(pl.multiple_of(i * BLOCK, BLOCK), BLOCK)
        key_rows = joint[:, pl.ds(pl.multiple_of(WIDTH + i * BLOCK, BLOCK), BLOCK)]
        values_ones[:, :BLOCK] = joint[:, pl.ds(pl.multiple_of(2 * WIDTH + i * BLOCK, BLOCK), BLOCK)]
        both = values_ones[...]
        for q in range(BLOCKS):
            rows = slice(q * BLOCK, (q + 1) * BLOCK)
            queries = joint[rows, columns]
            parts = []
            for h in range(2):
                scale = jnp.where(first == (h == 0), HEAD**-0.5, 0.0).astype(BF16)
                scores = matmul_nt(queries * scale, key_rows) + bias[rows, :]
                raised = jnp.exp(scores - jnp.max(scores, axis=1, keepdims=True))
                sums = matmul(raised.astype(BF16), both)
                parts.append(sums[:, :BLOCK] / sums[:, BLOCK:])
            context[rows, columns] = jnp.where(first, parts[0], parts[1]).astype(BF16)
        return carry

    lax.fori_loop(0, HEADS // 2, head_pair, 0)

    loads[3].wait()
    added = ordered[...].astype(F32) + matmul(context[...], w_out[...])
    hidden[...] = added.astype(BF16)
    moe_normed[...] = layer_norm(hidden[...].astype(F32)).astype(BF16)
    logits = matmul(moe_normed[...], keys)

    image = image_col[...]
    members = [image == float(s) for s in range(BLOCKS)]

    def by_image(per_image):
        chosen = per_image[0]
        for s in range(1, BLOCKS):
            chosen = jnp.where(members[s], per_image[s], chosen)
        return chosen

    column_max = [
        jnp.max(jnp.where(m, logits, NEGATIVE), axis=0, keepdims=True) for m in members
    ]
    raised = jnp.exp(logits - by_image(column_max))
    totals = [jnp.sum(jnp.where(m, raised, 0.0), axis=0, keepdims=True) for m in members]
    dispatch = jnp.transpose(raised / by_image(totals)).astype(BF16)

    halves = jnp.concatenate([moe_normed[:, :HALF], moe_normed[:, HALF:]], axis=0)
    image_row = segment & (BLOCKS - 1)
    eight = CHUNK * 8
    row = iota((eight, ROWS), 0)
    spread = one_hot(lax.broadcasted_iota(jnp.int32, (eight, CHUNK), 0) >> 3 == iota((eight, CHUNK), 1))
    own_image = ((row >> 1) & 3) == image_row

    def send_slots(k, carry):
        group = lax.div(k, GROUP_PEERS)
        pltpu.make_async_remote_copy(
            src_ref=slot_send.at[k], dst_ref=slot_recv.at[k],
            send_sem=slot_send_sem, recv_sem=slot_recv_sem.at[group],
            device_id=peer(k, 1), device_id_type=MESH,
        ).start()
        return carry

    for c in range(PEERS // CHUNK):
        wide = matmul(spread, dispatch[c * CHUNK : (c + 1) * CHUNK, :])
        weights = [
            jnp.where(own_image & ((row & 1) == h), wide, 0.0).astype(BF16) for h in range(2)
        ]
        summed = matmul(jnp.concatenate(weights, axis=1), halves)
        slot_send[c * CHUNK : (c + 1) * CHUNK] = summed.reshape(CHUNK, 8, HALF).astype(BF16)
        if c == 0:
            pltpu.make_async_copy(slot_send.at[0], slot_recv.at[0], slot_recv_sem.at[0]).start()
        lax.fori_loop(max(1, c * CHUNK), (c + 1) * CHUNK, send_slots, 0)

    top = jnp.exp(logits - jnp.max(logits, axis=1, keepdims=True))
    combine = (top / jnp.sum(top, axis=1, keepdims=True)).astype(BF16)
    column = iota((BLOCK, PEERS * 8), 1)
    repeat = one_hot(iota((PEERS, PEERS * 8), 1) >> 3 == iota((PEERS, PEERS * 8), 0))
    for q in range(BLOCKS):
        rows = slice(q * BLOCK, (q + 1) * BLOCK)
        wide = matmul(combine[rows, :], repeat)
        for c in range(PEERS * 8 // BLOCK):
            columns = slice(c * BLOCK, (c + 1) * BLOCK)
            slot = column[:, columns]
            own = ((slot >> 1) & 3).astype(F32) == image[rows, :]
            for h in range(2):
                mix_weights[h, rows, columns] = jnp.where(
                    own & ((slot & 1) == h), wide[:, columns], 0.0
                ).astype(BF16)

    def send_back(k, carry):
        group = lax.div(k, GROUP_PEERS)
        pltpu.make_async_remote_copy(
            src_ref=back_send.at[k], dst_ref=back_recv.at[k],
            send_sem=back_send_sem, recv_sem=back_recv_sem.at[group],
            device_id=peer(k, -1), device_id_type=MESH,
        ).start()
        return carry

    for load in loads[4:]:
        load.wait()
    four = CHUNK * 4
    pick = [one_hot(iota((four, eight), 1) == 2 * iota((four, eight), 0) + h) for h in range(2)]
    weave_q = iota((eight, eight), 1)
    weave = one_hot(
        iota((eight, eight), 0) == 2 * (weave_q & (four - 1)) + lax.shift_right_logical(weave_q, 7)
    )
    for g in range(GROUPS):
        group = slot_recv.at[pl.ds(g * GROUP_PEERS, GROUP_PEERS)]
        pltpu.make_async_copy(group, group, slot_recv_sem.at[g]).wait()
        for c in range(GROUP_PEERS // CHUNK):
            start = g * GROUP_PEERS + c * CHUNK
            arrived = slot_recv[start : start + CHUNK].reshape(eight, HALF)
            for h in range(2):
                rows_in[c * four : (c + 1) * four, h * HALF : (h + 1) * HALF] = matmul(
                    pick[h], arrived
                ).astype(BF16)
        left = rows_in[...]
        total = jnp.zeros((GROUP_PEERS * 4, WIDTH), F32)
        step = 512
        for c in range(HIDDEN // step):
            inner = gelu(matmul(left, w_up[:, c * step : (c + 1) * step])).astype(BF16)
            total = total + matmul(inner, w_down[c * step : (c + 1) * step, :])
        rows_out[...] = total.astype(BF16)
        for c in range(GROUP_PEERS // CHUNK):
            start = g * GROUP_PEERS + c * CHUNK
            rows = slice(c * four, (c + 1) * four)
            stacked = jnp.concatenate([rows_out[rows, :HALF], rows_out[rows, HALF:]], axis=0)
            back_send[start : start + CHUNK] = (
                matmul(weave, stacked).reshape(CHUNK, 8, HALF).astype(BF16)
            )
        if g == 0:
            pltpu.make_async_copy(back_send.at[0], back_recv.at[0], back_recv_sem.at[0]).start()
        lax.fori_loop(max(1, g * GROUP_PEERS), (g + 1) * GROUP_PEERS, send_back, 0)

    mixture = [jnp.zeros((ROWS, HALF), F32)] * 2
    for g in range(GROUPS):
        group = back_recv.at[pl.ds(g * GROUP_PEERS, GROUP_PEERS)]
        pltpu.make_async_copy(group, group, back_recv_sem.at[g]).wait()
        arrived = back_recv[g * GROUP_PEERS : (g + 1) * GROUP_PEERS].reshape(GROUP_PEERS * 8, HALF)
        columns = slice(g * GROUP_PEERS * 8, (g + 1) * GROUP_PEERS * 8)
        mixture = [mixture[h] + matmul(mix_weights[h, :, columns], arrived) for h in range(2)]
    for h in range(2):
        columns = slice(h * HALF, (h + 1) * HALF)
        result_ref[:, columns] = (hidden[:, columns].astype(F32) + mixture[h]).astype(BF16)

    sent = slot_send.at[pl.ds(1, PEERS - 1)]
    pltpu.make_async_copy(sent, sent, slot_send_sem).wait()
    sent = back_send.at[pl.ds(1, PEERS - 1)]
    pltpu.make_async_copy(sent, sent, back_send_sem).wait()


def per_device(
    patches, owner_slot, segment_ids, block_mask, project_in, project_out, slot_keys, expert_in, expert_out
):
    hbm, smem = pl.BlockSpec(memory_space=pl.ANY), pl.BlockSpec(memory_space=pltpu.SMEM)
    vmem = pl.BlockSpec(memory_space=pltpu.VMEM)
    exchange = pltpu.VMEM((PEERS, 8, HALF), BF16)
    dma = pltpu.SemaphoreType.DMA
    return pl.pallas_call(
        kernel,
        out_shape=jax.ShapeDtypeStruct((ROWS, WIDTH), BF16),
        in_specs=[hbm, smem, vmem, smem, hbm, hbm, hbm, hbm, hbm],
        out_specs=vmem,
        scratch_shapes=[
            pltpu.VMEM((BLOCKS, BLOCK, WIDTH), BF16),
            pltpu.VMEM((WIDTH, 3 * WIDTH), BF16),
            pltpu.VMEM((WIDTH, WIDTH), BF16),
            pltpu.VMEM((WIDTH, PEERS), BF16),
            pltpu.VMEM((WIDTH, HIDDEN), BF16),
            pltpu.VMEM((HIDDEN, WIDTH), BF16),
            pltpu.VMEM((DP, BLOCK, WIDTH), BF16),
            pltpu.VMEM((DP, BLOCK, WIDTH), BF16),
            pltpu.VMEM((DP, 8, 128), jnp.int32),
            pltpu.VMEM((DP, 8, 128), jnp.int32),
            pltpu.VMEM((ROWS, BLOCK), F32),
            pltpu.VMEM((ROWS, BLOCK), F32),
            pltpu.VMEM((ROWS, ROWS), F32),
            pltpu.VMEM((ROWS, WIDTH), BF16),
            pltpu.VMEM((ROWS, WIDTH), BF16),
            pltpu.VMEM((ROWS, 3 * WIDTH), BF16),
            pltpu.VMEM((ROWS, 2 * BLOCK), BF16),
            pltpu.VMEM((ROWS, WIDTH), BF16),
            pltpu.VMEM((ROWS, WIDTH), BF16),
            pltpu.VMEM((ROWS, WIDTH), BF16),
            exchange,
            exchange,
            exchange,
            exchange,
            pltpu.VMEM((GROUP_PEERS * 4, WIDTH), BF16),
            pltpu.VMEM((GROUP_PEERS * 4, WIDTH), BF16),
            pltpu.VMEM((2, ROWS, PEERS * 8), BF16),
            dma((6,)),
            dma((DP,)),
            dma((DP,)),
            dma((DP,)),
            dma((DP,)),
            dma,
            dma((GROUPS,)),
            dma,
            dma((GROUPS,)),
        ],
        compiler_params=pltpu.CompilerParams(
            collective_id=0, has_side_effects=True, vmem_limit_bytes=58 * 1024 * 1024
        ),
    )(
        patches.reshape(BLOCKS, BLOCK, WIDTH),
        owner_slot,
        segment_ids.reshape(1, ROWS),
        block_mask,
        project_in,
        project_out,
        slot_keys,
        expert_in,
        expert_out,
    )


def solution(mesh):
    in_specs = (
        P(("dp", "expert"), None),
        P(("dp", "expert")),
        P(("dp", "expert")),
        P(("dp", "expert"), None),
        P(),
        P(),
        P(),
        P(("dp", "expert"), None, None),
        P(("dp", "expert"), None, None),
    )
    return jax.shard_map(
        per_device,
        mesh=mesh,
        in_specs=in_specs,
        out_specs=P(("dp", "expert"), None),
        check_vma=False,
    )
```

profile of v0, /device:TPU:1, one launch (start us, length us, event | category | flops | bytes accessed | tf_op | source)
XLA Modules:
  0.0 77.2 jit_solution(13118083985930135566)
XLA Ops:
  0.0 75.1 %shard_map.91 = bf16[512,768]{1,0:T(8,128)(2,1)} custom-call(bf16[4,128,768]{2,1,0:T(8,128)(2,1)} %bitcast.2, s32[4]{0:T(128)} %owner_ref.1, s32[1,512]{1,0:T(1,128)} %bitcast.3, s32[4,4]{1,0:T(4,128)} %mask_ref.1, bf16[768,2304]{1,0:T(8,128)(2,1)} %in_hbm.1, bf16[768,768]{1,0:T(8,128)(2,1)} %out_hbm.1, bf16[768,128]{1,0:T(8,128)(2,1)} %keys_hbm.1, ...), custom_call_target="tpu_custom_call" | custom-call | tf_op jit(solution)/shard_map/pallas_call | solution.py:336
  75.1 2.1 %copy.11 = bf16[512,768]{1,0:T(8,128)(2,1)} copy(bf16[512,768]{1,0:T(8,128)(2,1)} %shard_map.91) | data formatting | bytes 1572864
where the time goes:
time: 77.4 us; the launch traced here: 77.2 us
  Pallas kernels  75.1 us (97%)
  local copies, waits for them, and re-layouts  2.06 us (3%)
    pallas_call x1, Pallas kernels, per_device(): pl.pallas_call(kernel, out_shape=jax.ShapeDtypeStruct((ROWS, WIDTH), BF16...  75.1 us
    unnamed x1, local copies, waits for them, and re-layouts  2.06 us

commit v1 on v0

--- a/solution.py
+++ b/solution.py
@@ -61,31 +61,30 @@
     seg_col, image_col, bias, ordered, normed, joint, values_ones, context, hidden, moe_normed,
     slot_send, slot_recv, back_send, back_recv, rows_in, rows_out, mix_weights,
     load_sem, block_send_sem, block_recv_sem, place_send_sem, place_recv_sem,
-    slot_send_sem, slot_recv_sem, back_send_sem, back_recv_sem,
+    slot_send_sem, slot_recv_sem, back_send_sem, back_recv_sem, plane_sem, cube_sem,
 ):
     dp, ex = lax.axis_index("dp"), lax.axis_index("expert")
     y, core = lax.div(dp, 2), lax.rem(dp, 2)
     z, x = lax.div(ex, 4), lax.rem(ex, 4)
 
-    def ahead(k):
-        ax = lax.rem(k, 4)
-        az = lax.rem(lax.div(k, 4) + ax, 4)
-        ay = lax.rem(lax.div(k, 16) + ax, 4)
-        return ax, ay, az, lax.div(k, 64)
+    dp_at = [[lax.rem(y + ay, 4) * 2 + lax.rem(core + ac, 2) for ac in range(2)] for ay in range(4)]
+    ex_at = [[lax.rem(z + az, 4) * 4 + lax.rem(x + ax, 4) for ax in range(4)] for az in range(4)]
 
     def peer(k, sign):
-        ax, ay, az, ac = ahead(k)
-        to_y, to_c = lax.rem(y + sign * ay + 4, 4), lax.rem(core + ac, 2)
-        to_z, to_x = lax.rem(z + sign * az + 4, 4), lax.rem(x + sign * ax + 4, 4)
-        return (to_y * 2 + to_c, to_z * 4 + to_x)
+        ax = k % 4
+        ay, az, ac = (k // 16 + ax) % 4, (k // 4 + ax) % 4, k // 64
+        return (dp_at[sign * ay % 4][ac], ex_at[sign * az % 4][sign * ax % 4])
 
     barrier = pltpu.get_barrier_semaphore()
-
-    def greet(k, carry):
-        pl.semaphore_signal(barrier, inc=1, device_id=peer(k, 1), device_id_type=MESH)
-        return carry
-
-    lax.fori_loop(1, PEERS, greet, 0)
+    line_dp = [(dp_at[a % 4][a // 4], ex) for a in range(1, DP)]
+    line_z = [(dp, ex_at[a][0]) for a in range(1, 4)]
+    line_x = [(dp, ex_at[0][a]) for a in range(1, 4)]
+
+    def tell(semaphore, line):
+        for device in line:
+            pl.semaphore_signal(semaphore, inc=1, device_id=device, device_id_type=MESH)
+
+    tell(barrier, line_dp + line_z + line_x)
 
     loads = [
         pltpu.make_async_copy(source, target, load_sem.at[i])
@@ -106,12 +105,9 @@
     targets = [lax.div(owner_ref[b], BLOCKS * PEERS // DP) for b in range(BLOCKS)]
     places = [lax.rem(owner_ref[b], BLOCKS) for b in range(BLOCKS)]
 
-    def dp_peer(a, sign):
-        return lax.rem(y + sign * (a % 4) + 4, 4) * 2 + lax.rem(core + a // 4, 2)
-
     loads[0].wait()
     for a in range(DP):
-        to = dp_peer(a, 1)
+        to = dp_at[a % 4][a // 4]
         index, place = jnp.int32(0), jnp.int32(-1)
         for b in range(BLOCKS):
             hit = targets[b] == to
@@ -124,10 +120,10 @@
             slots[0] = patches[index]
             place_in[0] = jnp.full((8, 128), place, jnp.int32)
 
-    pl.semaphore_wait(barrier, PEERS - 1)
+    pl.semaphore_wait(barrier, 13)
     sends = []
     for a in (2, 6, 1, 3, 5, 7, 4):
-        to = (dp_peer(a, 1), ex)
+        to = (dp_at[a % 4][a // 4], ex)
         for source, target, send, recv in (
             (place_out, place_in, place_send_sem, place_recv_sem),
             (stage, slots, block_send_sem, block_recv_sem),
@@ -139,6 +135,7 @@
             copy.start()
             sends.append(copy)
 
+    tell(plane_sem, line_x)
     segment = segment_ref[...]
     seg_col[...] = jnp.transpose(jnp.broadcast_to(segment.astype(F32), (BLOCK, ROWS)))
     image_col[...] = jnp.transpose(
@@ -152,6 +149,8 @@
             bias[rows, columns] = jnp.where(same, link, NEGATIVE)
     values_ones[:, BLOCK:] = jnp.ones((ROWS, BLOCK), BF16)
 
+    pl.semaphore_wait(plane_sem, 3)
+    tell(cube_sem, line_dp)
     k_lane = iota((PEERS, PEERS), 1)
     ax = k_lane & 3
     az = ((k_lane >> 2) + ax) & 3
@@ -165,6 +164,7 @@
 
     for copy in sends:
         copy.wait()
+    pl.semaphore_wait(cube_sem, DP - 1)
     for p in range(BLOCKS):
         where_from = jnp.zeros((8, 128), jnp.int32)
         for a in range(1, DP):
@@ -228,14 +228,15 @@
     spread = one_hot(lax.broadcasted_iota(jnp.int32, (eight, CHUNK), 0) >> 3 == iota((eight, CHUNK), 1))
     own_image = ((row >> 1) & 3) == image_row
 
-    def send_slots(k, carry):
-        group = lax.div(k, GROUP_PEERS)
-        pltpu.make_async_remote_copy(
-            src_ref=slot_send.at[k], dst_ref=slot_recv.at[k],
-            send_sem=slot_send_sem, recv_sem=slot_recv_sem.at[group],
-            device_id=peer(k, 1), device_id_type=MESH,
-        ).start()
-        return carry
+    def send(k, source, target, send_sem, recv_sem, sign):
+        recv = recv_sem.at[k // GROUP_PEERS]
+        if k:
+            pltpu.make_async_remote_copy(
+                src_ref=source.at[k], dst_ref=target.at[k], send_sem=send_sem, recv_sem=recv,
+                device_id=peer(k, sign), device_id_type=MESH,
+            ).start()
+        else:
+            pltpu.make_async_copy(source.at[0], target.at[0], recv).start()
 
     for c in range(PEERS // CHUNK):
         wide = matmul(spread, dispatch[c * CHUNK : (c + 1) * CHUNK, :])
@@ -244,9 +245,8 @@
         ]
         summed = matmul(jnp.concatenate(weights, axis=1), halves)
         slot_send[c * CHUNK : (c + 1) * CHUNK] = summed.reshape(CHUNK, 8, HALF).astype(BF16)
-        if c == 0:
-            pltpu.make_async_copy(slot_send.at[0], slot_recv.at[0], slot_recv_sem.at[0]).start()
-        lax.fori_loop(max(1, c * CHUNK), (c + 1) * CHUNK, send_slots, 0)
+        for k in range(c * CHUNK, (c + 1) * CHUNK):
+            send(k, slot_send, slot_recv, slot_send_sem, slot_recv_sem, 1)
 
     top = jnp.exp(logits - jnp.max(logits, axis=1, keepdims=True))
     combine = (top / jnp.sum(top, axis=1, keepdims=True)).astype(BF16)
@@ -263,15 +263,6 @@
                 mix_weights[h, rows, columns] = jnp.where(
                     own & ((slot & 1) == h), wide[:, columns], 0.0
                 ).astype(BF16)
-
-    def send_back(k, carry):
-        group = lax.div(k, GROUP_PEERS)
-        pltpu.make_async_remote_copy(
-            src_ref=back_send.at[k], dst_ref=back_recv.at[k],
-            send_sem=back_send_sem, recv_sem=back_recv_sem.at[group],
-            device_id=peer(k, -1), device_id_type=MESH,
-        ).start()
-        return carry
 
     for load in loads[4:]:
         load.wait()
@@ -305,9 +296,8 @@
             back_send[start : start + CHUNK] = (
                 matmul(weave, stacked).reshape(CHUNK, 8, HALF).astype(BF16)
             )
-        if g == 0:
-            pltpu.make_async_copy(back_send.at[0], back_recv.at[0], back_recv_sem.at[0]).start()
-        lax.fori_loop(max(1, g * GROUP_PEERS), (g + 1) * GROUP_PEERS, send_back, 0)
+        for k in range(g * GROUP_PEERS, (g + 1) * GROUP_PEERS):
+            send(k, back_send, back_recv, back_send_sem, back_recv_sem, -1)
 
     mixture = [jnp.zeros((ROWS, HALF), F32)] * 2
     for g in range(GROUPS):
@@ -375,6 +365,8 @@
             dma((GROUPS,)),
             dma,
             dma((GROUPS,)),
+            pltpu.SemaphoreType.REGULAR,
+            pltpu.SemaphoreType.REGULAR,
         ],
         compiler_params=pltpu.CompilerParams(
             collective_id=0, has_side_effects=True, vmem_limit_bytes=58 * 1024 * 1024

time: 77.4 us -> 69.5 us (0.90)
  Pallas kernels: 75.1 us -> 67.3 us
    pallas_call x1, Pallas kernels: 75.1 us -> 67.3 us  [per_device(): pl.pallas_call(kernel, out_shape=jax.ShapeDtypeStruct((ROWS, WIDTH), BF16...]
where the time goes in v1:
time: 69.5 us; the launch traced here: 69.3 us
  Pallas kernels  67.3 us (97%)
  local copies, waits for them, and re-layouts  2.06 us (3%)
    pallas_call x1, Pallas kernels, per_device(): pl.pallas_call(kernel, out_shape=jax.ShapeDtypeStruct((ROWS, WIDTH), BF16...  67.3 us
    unnamed x1, local copies, waits for them, and re-layouts  2.06 us

profile of v1, /device:TPU:1, one launch (start us, length us, event | category | flops | bytes accessed | tf_op | source)
XLA Modules:
  0.0 69.3 jit_solution(13221159645662643180)
XLA Ops:
  0.0 67.3 %shard_map.91 = bf16[512,768]{1,0:T(8,128)(2,1)} custom-call(bf16[4,128,768]{2,1,0:T(8,128)(2,1)} %bitcast.2, s32[4]{0:T(128)} %owner_ref.1, s32[1,512]{1,0:T(1,128)} %bitcast.3, s32[4,4]{1,0:T(4,128)} %mask_ref.1, bf16[768,2304]{1,0:T(8,128)(2,1)} %in_hbm.1, bf16[768,768]{1,0:T(8,128)(2,1)} %out_hbm.1, bf16[768,128]{1,0:T(8,128)(2,1)} %keys_hbm.1, ...), custom_call_target="tpu_custom_call" | custom-call | tf_op jit(solution)/shard_map/pallas_call | solution.py:326
  67.3 2.1 %copy.11 = bf16[512,768]{1,0:T(8,128)(2,1)} copy(bf16[512,768]{1,0:T(8,128)(2,1)} %shard_map.91) | data formatting | bytes 1572864

commit v2 on v1

--- a/solution.py
+++ b/solution.py
@@ -17,9 +17,9 @@
 PEERS = 128
 EPS = 1e-06
 NEGATIVE = -1e30
-GROUPS = 2
-GROUP_PEERS = PEERS // GROUPS
+GROUPS = ((0, 32), (32, 32), (64, 32), (96, 32))
 CHUNK = 32
+ORDER = (4, 2, 6, 1, 3, 5, 7)
 MESH = pl.DeviceIdType.MESH
 F32 = jnp.float32
 BF16 = jnp.bfloat16
@@ -58,7 +58,7 @@
     result_ref,
     patches, w_in, w_out, w_keys, w_up, w_down,
     stage, slots, place_out, place_in,
-    seg_col, image_col, bias, ordered, normed, joint, values_ones, context, hidden, moe_normed,
+    seg_col, image_col, bias, arrived_joint, context, hidden, moe_normed,
     slot_send, slot_recv, back_send, back_recv, rows_in, rows_out, mix_weights,
     load_sem, block_send_sem, block_recv_sem, place_send_sem, place_recv_sem,
     slot_send_sem, slot_recv_sem, back_send_sem, back_recv_sem, plane_sem, cube_sem,
@@ -121,8 +121,8 @@
             place_in[0] = jnp.full((8, 128), place, jnp.int32)
 
     pl.semaphore_wait(barrier, 13)
-    sends = []
-    for a in (2, 6, 1, 3, 5, 7, 4):
+    sends = {}
+    for a in ORDER:
         to = (dp_at[a % 4][a // 4], ex)
         for source, target, send, recv in (
             (place_out, place_in, place_send_sem, place_recv_sem),
@@ -133,7 +133,7 @@
                 device_id=to, device_id_type=MESH,
             )
             copy.start()
-            sends.append(copy)
+            sends.setdefault(a, []).append(copy)
 
     tell(plane_sem, line_x)
     segment = segment_ref[...]
@@ -147,7 +147,6 @@
             rows, columns = slice(a * BLOCK, (a + 1) * BLOCK), slice(b * BLOCK, (b + 1) * BLOCK)
             same = seg_col[rows, :] == segment[:, columns].astype(F32)
             bias[rows, columns] = jnp.where(same, link, NEGATIVE)
-    values_ones[:, BLOCK:] = jnp.ones((ROWS, BLOCK), BF16)
 
     pl.semaphore_wait(plane_sem, 3)
     tell(cube_sem, line_dp)
@@ -162,45 +161,56 @@
         load.wait()
     keys = matmul(w_keys[...], reorder).astype(BF16)
 
-    for copy in sends:
-        copy.wait()
+    def arrive(a):
+        rows = layer_norm(slots[a].astype(F32)).astype(BF16)
+        for c in range(3):
+            columns = slice(c * WIDTH, (c + 1) * WIDTH)
+            arrived_joint[a, :, columns] = matmul(rows, w_in[:, columns]).astype(BF16)
+
+    arrive(0)
+    for a in ORDER:
+        for copy in sends[a]:
+            copy.wait()
+        arrive(a)
     pl.semaphore_wait(cube_sem, DP - 1)
+    source = []
     for p in range(BLOCKS):
         where_from = jnp.zeros((8, 128), jnp.int32)
         for a in range(1, DP):
             where_from = jnp.where(place_in[a] == p, a, where_from)
-        index = jnp.max(where_from)
-        block = slots[index]
-        rows = slice(p * BLOCK, (p + 1) * BLOCK)
-        ordered[rows, :] = block
-        normed[rows, :] = layer_norm(block.astype(F32)).astype(BF16)
-    joint[...] = matmul(normed[...], w_in[...]).astype(BF16)
+        source.append(jnp.max(where_from))
 
     lane = iota((BLOCK, BLOCK), 1)
     first = lane < HEAD
-
-    def head_pair(i, carry):
-        columns = pl.ds(pl.multiple_of(i * BLOCK, BLOCK), BLOCK)
-        key_rows = joint[:, pl.ds(pl.multiple_of(WIDTH + i * BLOCK, BLOCK), BLOCK)]
-        values_ones[:, :BLOCK] = joint[:, pl.ds(pl.multiple_of(2 * WIDTH + i * BLOCK, BLOCK), BLOCK)]
-        both = values_ones[...]
+    scales = [jnp.where(first == (h == 0), HEAD**-0.5, 0.0).astype(BF16) for h in range(2)]
+
+    ones = jnp.ones((ROWS, BLOCK), BF16)
+    for i in range(HEADS // 2):
+        columns = slice(i * BLOCK, (i + 1) * BLOCK)
+
+        def placed(part):
+            at = slice(part * WIDTH + i * BLOCK, part * WIDTH + (i + 1) * BLOCK)
+            return [arrived_joint[index, :, at] for index in source]
+
+        query_blocks = placed(0)
+        key_rows = jnp.concatenate(placed(1), axis=0)
+        both = jnp.concatenate([jnp.concatenate(placed(2), axis=0), ones], axis=1)
         for q in range(BLOCKS):
             rows = slice(q * BLOCK, (q + 1) * BLOCK)
-            queries = joint[rows, columns]
-            parts = []
+            queries = query_blocks[q]
+            stacked = jnp.concatenate([queries * scale for scale in scales], axis=0)
+            scores = matmul_nt(stacked, key_rows)
+            raised = []
             for h in range(2):
-                scale = jnp.where(first == (h == 0), HEAD**-0.5, 0.0).astype(BF16)
-                scores = matmul_nt(queries * scale, key_rows) + bias[rows, :]
-                raised = jnp.exp(scores - jnp.max(scores, axis=1, keepdims=True))
-                sums = matmul(raised.astype(BF16), both)
-                parts.append(sums[:, :BLOCK] / sums[:, BLOCK:])
-            context[rows, columns] = jnp.where(first, parts[0], parts[1]).astype(BF16)
-        return carry
-
-    lax.fori_loop(0, HEADS // 2, head_pair, 0)
+                linked = scores[h * BLOCK : (h + 1) * BLOCK, :] + bias[rows, :]
+                raised.append(jnp.exp(linked - jnp.max(linked, axis=1, keepdims=True)).astype(BF16))
+            sums = matmul(jnp.concatenate(raised, axis=0), both)
+            parts = sums[:, :BLOCK] / sums[:, BLOCK:]
+            context[rows, columns] = jnp.where(first, parts[:BLOCK], parts[BLOCK:]).astype(BF16)
 
     loads[3].wait()
-    added = ordered[...].astype(F32) + matmul(context[...], w_out[...])
+    ordered = jnp.concatenate([slots[index] for index in source], axis=0)
+    added = ordered.astype(F32) + matmul(context[...], w_out[...])
     hidden[...] = added.astype(BF16)
     moe_normed[...] = layer_norm(hidden[...].astype(F32)).astype(BF16)
     logits = matmul(moe_normed[...], keys)
@@ -229,7 +239,7 @@
     own_image = ((row >> 1) & 3) == image_row
 
     def send(k, source, target, send_sem, recv_sem, sign):
-        recv = recv_sem.at[k // GROUP_PEERS]
+        recv = recv_sem.at[sum(k >= first + count for first, count in GROUPS)]
         if k:
             pltpu.make_async_remote_copy(
                 src_ref=source.at[k], dst_ref=target.at[k], send_sem=send_sem, recv_sem=recv,
@@ -272,39 +282,39 @@
     weave = one_hot(
         iota((eight, eight), 0) == 2 * (weave_q & (four - 1)) + lax.shift_right_logical(weave_q, 7)
     )
-    for g in range(GROUPS):
-        group = slot_recv.at[pl.ds(g * GROUP_PEERS, GROUP_PEERS)]
+    for g, (begin, count) in enumerate(GROUPS):
+        group = slot_recv.at[pl.ds(begin, count)]
         pltpu.make_async_copy(group, group, slot_recv_sem.at[g]).wait()
-        for c in range(GROUP_PEERS // CHUNK):
-            start = g * GROUP_PEERS + c * CHUNK
+        for c in range(count // CHUNK):
+            start = begin + c * CHUNK
             arrived = slot_recv[start : start + CHUNK].reshape(eight, HALF)
             for h in range(2):
                 rows_in[c * four : (c + 1) * four, h * HALF : (h + 1) * HALF] = matmul(
                     pick[h], arrived
                 ).astype(BF16)
-        left = rows_in[...]
-        total = jnp.zeros((GROUP_PEERS * 4, WIDTH), F32)
+        left = rows_in[: count * 4, :]
+        total = jnp.zeros((count * 4, WIDTH), F32)
         step = 512
         for c in range(HIDDEN // step):
             inner = gelu(matmul(left, w_up[:, c * step : (c + 1) * step])).astype(BF16)
             total = total + matmul(inner, w_down[c * step : (c + 1) * step, :])
-        rows_out[...] = total.astype(BF16)
-        for c in range(GROUP_PEERS // CHUNK):
-            start = g * GROUP_PEERS + c * CHUNK
+        rows_out[: count * 4, :] = total.astype(BF16)
+        for c in range(count // CHUNK):
+            start = begin + c * CHUNK
             rows = slice(c * four, (c + 1) * four)
             stacked = jnp.concatenate([rows_out[rows, :HALF], rows_out[rows, HALF:]], axis=0)
             back_send[start : start + CHUNK] = (
                 matmul(weave, stacked).reshape(CHUNK, 8, HALF).astype(BF16)
             )
-        for k in range(g * GROUP_PEERS, (g + 1) * GROUP_PEERS):
+        for k in range(begin, begin + count):
             send(k, back_send, back_recv, back_send_sem, back_recv_sem, -1)
 
     mixture = [jnp.zeros((ROWS, HALF), F32)] * 2
-    for g in range(GROUPS):
-        group = back_recv.at[pl.ds(g * GROUP_PEERS, GROUP_PEERS)]
+    for g, (begin, count) in enumerate(GROUPS):
+        group = back_recv.at[pl.ds(begin, count)]
         pltpu.make_async_copy(group, group, back_recv_sem.at[g]).wait()
-        arrived = back_recv[g * GROUP_PEERS : (g + 1) * GROUP_PEERS].reshape(GROUP_PEERS * 8, HALF)
-        columns = slice(g * GROUP_PEERS * 8, (g + 1) * GROUP_PEERS * 8)
+        arrived = back_recv[begin : begin + count].reshape(count * 8, HALF)
+        columns = slice(begin * 8, (begin + count) * 8)
         mixture = [mixture[h] + matmul(mix_weights[h, :, columns], arrived) for h in range(2)]
     for h in range(2):
         columns = slice(h * HALF, (h + 1) * HALF)
@@ -342,10 +352,7 @@
             pltpu.VMEM((ROWS, BLOCK), F32),
             pltpu.VMEM((ROWS, BLOCK), F32),
             pltpu.VMEM((ROWS, ROWS), F32),
-            pltpu.VMEM((ROWS, WIDTH), BF16),
-            pltpu.VMEM((ROWS, WIDTH), BF16),
-            pltpu.VMEM((ROWS, 3 * WIDTH), BF16),
-            pltpu.VMEM((ROWS, 2 * BLOCK), BF16),
+            pltpu.VMEM((DP, BLOCK, 3 * WIDTH), BF16),
             pltpu.VMEM((ROWS, WIDTH), BF16),
             pltpu.VMEM((ROWS, WIDTH), BF16),
             pltpu.VMEM((ROWS, WIDTH), BF16),
@@ -353,8 +360,8 @@
             exchange,
             exchange,
             exchange,
-            pltpu.VMEM((GROUP_PEERS * 4, WIDTH), BF16),
-            pltpu.VMEM((GROUP_PEERS * 4, WIDTH), BF16),
+            pltpu.VMEM((max(n for _, n in GROUPS) * 4, WIDTH), BF16),
+            pltpu.VMEM((max(n for _, n in GROUPS) * 4, WIDTH), BF16),
             pltpu.VMEM((2, ROWS, PEERS * 8), BF16),
             dma((6,)),
             dma((DP,)),
@@ -362,9 +369,9 @@
             dma((DP,)),
             dma((DP,)),
             dma,
-            dma((GROUPS,)),
+            dma((len(GROUPS),)),
             dma,
-            dma((GROUPS,)),
+            dma((len(GROUPS),)),
             pltpu.SemaphoreType.REGULAR,
             pltpu.SemaphoreType.REGULAR,
         ],

time: 69.5 us -> 63.5 us (0.914)
  Pallas kernels: 67.3 us -> 61.3 us
    pallas_call x1, Pallas kernels: 67.3 us -> 61.3 us  [per_device(): pl.pallas_call(kernel, out_shape=jax.ShapeDtypeStruct((ROWS, WIDTH), BF16...]
where the time goes in v2:
time: 63.5 us; the launch traced here: 63.4 us
  Pallas kernels  61.3 us (97%)
  local copies, waits for them, and re-layouts  2.06 us (3%)
    pallas_call x1, Pallas kernels, per_device(): pl.pallas_call(kernel, out_shape=jax.ShapeDtypeStruct((ROWS, WIDTH), BF16...  61.3 us
    unnamed x1, local copies, waits for them, and re-layouts  2.06 us

profile of v2, /device:TPU:1, one launch (start us, length us, event | category | flops | bytes accessed | tf_op | source)
XLA Modules:
  0.0 63.4 jit_solution(10533515675802444596)
XLA Ops:
  0.0 61.3 %shard_map.91 = bf16[512,768]{1,0:T(8,128)(2,1)} custom-call(bf16[4,128,768]{2,1,0:T(8,128)(2,1)} %bitcast.2, s32[4]{0:T(128)} %owner_ref.1, s32[1,512]{1,0:T(1,128)} %bitcast.3, s32[4,4]{1,0:T(4,128)} %mask_ref.1, bf16[768,2304]{1,0:T(8,128)(2,1)} %in_hbm.1, bf16[768,768]{1,0:T(8,128)(2,1)} %out_hbm.1, bf16[768,128]{1,0:T(8,128)(2,1)} %keys_hbm.1, ...), custom_call_target="tpu_custom_call" | custom-call | tf_op jit(solution)/shard_map/pallas_call | solution.py:336
  61.3 2.1 %copy.11 = bf16[512,768]{1,0:T(8,128)(2,1)} copy(bf16[512,768]{1,0:T(8,128)(2,1)} %shard_map.91) | data formatting | bytes 1572864

commit v3 on v2

--- a/solution.py
+++ b/solution.py
@@ -258,6 +258,41 @@
         for k in range(c * CHUNK, (c + 1) * CHUNK):
             send(k, slot_send, slot_recv, slot_send_sem, slot_recv_sem, 1)
 
+    for load in loads[4:]:
+        load.wait()
+    four = CHUNK * 4
+    pick = [one_hot(iota((four, eight), 1) == 2 * iota((four, eight), 0) + h) for h in range(2)]
+    weave_q = iota((eight, eight), 1)
+    weave = one_hot(
+        iota((eight, eight), 0) == 2 * (weave_q & (four - 1)) + lax.shift_right_logical(weave_q, 7)
+    )
+    for g, (begin, count) in enumerate(GROUPS):
+        group = slot_recv.at[pl.ds(begin, count)]
+        pltpu.make_async_copy(group, group, slot_recv_sem.at[g]).wait()
+        for c in range(count // CHUNK):
+            start = begin + c * CHUNK
+            arrived = slot_recv[start : start + CHUNK].reshape(eight, HALF)
+            for h in range(2):
+                rows_in[c * four : (c + 1) * four, h * HALF : (h + 1) * HALF] = matmul(
+                    pick[h], arrived
+                ).astype(BF16)
+        left = rows_in[: count * 4, :]
+        total = jnp.zeros((count * 4, WIDTH), F32)
+        step = 1536
+        for c in range(HIDDEN // step):
+            inner = gelu(matmul(left, w_up[:, c * step : (c + 1) * step])).astype(BF16)
+            total = total + matmul(inner, w_down[c * step : (c + 1) * step, :])
+        rows_out[: count * 4, :] = total.astype(BF16)
+        for c in range(count // CHUNK):
+            start = begin + c * CHUNK
+            rows = slice(c * four, (c + 1) * four)
+            stacked = jnp.concatenate([rows_out[rows, :HALF], rows_out[rows, HALF:]], axis=0)
+            back_send[start : start + CHUNK] = (
+                matmul(weave, stacked).reshape(CHUNK, 8, HALF).astype(BF16)
+            )
+        for k in range(begin, begin + count):
+            send(k, back_send, back_recv, back_send_sem, back_recv_sem, -1)
+
     top = jnp.exp(logits - jnp.max(logits, axis=1, keepdims=True))
     combine = (top / jnp.sum(top, axis=1, keepdims=True)).astype(BF16)
     column = iota((BLOCK, PEERS * 8), 1)
@@ -273,41 +308,6 @@
                 mix_weights[h, rows, columns] = jnp.where(
                     own & ((slot & 1) == h), wide[:, columns], 0.0
                 ).astype(BF16)
-
-    for load in loads[4:]:
-        load.wait()
-    four = CHUNK * 4
-    pick = [one_hot(iota((four, eight), 1) == 2 * iota((four, eight), 0) + h) for h in range(2)]
-    weave_q = iota((eight, eight), 1)
-    weave = one_hot(
-        iota((eight, eight), 0) == 2 * (weave_q & (four - 1)) + lax.shift_right_logical(weave_q, 7)
-    )
-    for g, (begin, count) in enumerate(GROUPS):
-        group = slot_recv.at[pl.ds(begin, count)]
-        pltpu.make_async_copy(group, group, slot_recv_sem.at[g]).wait()
-        for c in range(count // CHUNK):
-            start = begin + c * CHUNK
-            arrived = slot_recv[start : start + CHUNK].reshape(eight, HALF)
-            for h in range(2):
-                rows_in[c * four : (c + 1) * four, h * HALF : (h + 1) * HALF] = matmul(
-                    pick[h], arrived
-                ).astype(BF16)
-        left = rows_in[: count * 4, :]
-        total = jnp.zeros((count * 4, WIDTH), F32)
-        step = 512
-        for c in range(HIDDEN // step):
-            inner = gelu(matmul(left, w_up[:, c * step : (c + 1) * step])).astype(BF16)
-            total = total + matmul(inner, w_down[c * step : (c + 1) * step, :])
-        rows_out[: count * 4, :] = total.astype(BF16)
-        for c in range(count // CHUNK):
-            start = begin + c * CHUNK
-            rows = slice(c * four, (c + 1) * four)
-            stacked = jnp.concatenate([rows_out[rows, :HALF], rows_out[rows, HALF:]], axis=0)
-            back_send[start : start + CHUNK] = (
-                matmul(weave, stacked).reshape(CHUNK, 8, HALF).astype(BF16)
-            )
-        for k in range(begin, begin + count):
-            send(k, back_send, back_recv, back_send_sem, back_recv_sem, -1)
 
     mixture = [jnp.zeros((ROWS, HALF), F32)] * 2
     for g, (begin, count) in enumerate(GROUPS):

time: 63.5 us -> 62.9 us (level)
  no operation moved by 1% of the time
where the time goes in v3:
time: 62.9 us; the launch traced here: 62.7 us
  Pallas kernels  60.7 us (97%)
  local copies, waits for them, and re-layouts  2.06 us (3%)
    pallas_call x1, Pallas kernels, per_device(): pl.pallas_call(kernel, out_shape=jax.ShapeDtypeStruct((ROWS, WIDTH), BF16...  60.7 us
    unnamed x1, local copies, waits for them, and re-layouts  2.06 us

profile of v3, /device:TPU:1, one launch (start us, length us, event | category | flops | bytes accessed | tf_op | source)
XLA Modules:
  0.0 62.7 jit_solution(3939840578972806372)
XLA Ops:
  0.0 60.7 %shard_map.91 = bf16[512,768]{1,0:T(8,128)(2,1)} custom-call(bf16[4,128,768]{2,1,0:T(8,128)(2,1)} %bitcast.2, s32[4]{0:T(128)} %owner_ref.1, s32[1,512]{1,0:T(1,128)} %bitcast.3, s32[4,4]{1,0:T(4,128)} %mask_ref.1, bf16[768,2304]{1,0:T(8,128)(2,1)} %in_hbm.1, bf16[768,768]{1,0:T(8,128)(2,1)} %out_hbm.1, bf16[768,128]{1,0:T(8,128)(2,1)} %keys_hbm.1, ...), custom_call_target="tpu_custom_call" | custom-call | tf_op jit(solution)/shard_map/pallas_call | solution.py:336
  60.7 2.1 %copy.11 = bf16[512,768]{1,0:T(8,128)(2,1)} copy(bf16[512,768]{1,0:T(8,128)(2,1)} %shard_map.91) | data formatting | bytes 1572864

commit v4 on v3

--- a/solution.py
+++ b/solution.py
@@ -19,7 +19,7 @@
 NEGATIVE = -1e30
 GROUPS = ((0, 32), (32, 32), (64, 32), (96, 32))
 CHUNK = 32
-ORDER = (4, 2, 6, 1, 3, 5, 7)
+ORDER = (2, 1, 3, 4, 6, 5, 7)
 MESH = pl.DeviceIdType.MESH
 F32 = jnp.float32
 BF16 = jnp.bfloat16

time: 62.9 us -> 63 us (level)
  no operation moved by 1% of the time
where the time goes in v4:
time: 63 us; the launch traced here: 62.8 us
  Pallas kernels  60.8 us (97%)
  local copies, waits for them, and re-layouts  2.06 us (3%)
    pallas_call x1, Pallas kernels, per_device(): pl.pallas_call(kernel, out_shape=jax.ShapeDtypeStruct((ROWS, WIDTH), BF16...  60.8 us
    unnamed x1, local copies, waits for them, and re-layouts  2.06 us

profile of v4, /device:TPU:1, one launch (start us, length us, event | category | flops | bytes accessed | tf_op | source)
XLA Modules:
  0.0 62.8 jit_solution(7021047540555713665)
XLA Ops:
  0.0 60.8 %shard_map.91 = bf16[512,768]{1,0:T(8,128)(2,1)} custom-call(bf16[4,128,768]{2,1,0:T(8,128)(2,1)} %bitcast.2, s32[4]{0:T(128)} %owner_ref.1, s32[1,512]{1,0:T(1,128)} %bitcast.3, s32[4,4]{1,0:T(4,128)} %mask_ref.1, bf16[768,2304]{1,0:T(8,128)(2,1)} %in_hbm.1, bf16[768,768]{1,0:T(8,128)(2,1)} %out_hbm.1, bf16[768,128]{1,0:T(8,128)(2,1)} %keys_hbm.1, ...), custom_call_target="tpu_custom_call" | custom-call | tf_op jit(solution)/shard_map/pallas_call | solution.py:336
  60.8 2.1 %copy.11 = bf16[512,768]{1,0:T(8,128)(2,1)} copy(bf16[512,768]{1,0:T(8,128)(2,1)} %shard_map.91) | data formatting | bytes 1572864

commit v5 on v3

--- a/solution.py
+++ b/solution.py
@@ -180,7 +180,7 @@
             where_from = jnp.where(place_in[a] == p, a, where_from)
         source.append(jnp.max(where_from))
 
-    lane = iota((BLOCK, BLOCK), 1)
+    lane = iota((2 * BLOCK, BLOCK), 1)
     first = lane < HEAD
     scales = [jnp.where(first == (h == 0), HEAD**-0.5, 0.0).astype(BF16) for h in range(2)]
 
@@ -195,18 +195,18 @@
         query_blocks = placed(0)
         key_rows = jnp.concatenate(placed(1), axis=0)
         both = jnp.concatenate([jnp.concatenate(placed(2), axis=0), ones], axis=1)
-        for q in range(BLOCKS):
-            rows = slice(q * BLOCK, (q + 1) * BLOCK)
-            queries = query_blocks[q]
+        for q in (0, 2):
+            rows, pair = slice(q * BLOCK, (q + 2) * BLOCK), 2 * BLOCK
+            queries = jnp.concatenate(query_blocks[q : q + 2], axis=0)
             stacked = jnp.concatenate([queries * scale for scale in scales], axis=0)
             scores = matmul_nt(stacked, key_rows)
             raised = []
             for h in range(2):
-                linked = scores[h * BLOCK : (h + 1) * BLOCK, :] + bias[rows, :]
+                linked = scores[h * pair : (h + 1) * pair, :] + bias[rows, :]
                 raised.append(jnp.exp(linked - jnp.max(linked, axis=1, keepdims=True)).astype(BF16))
             sums = matmul(jnp.concatenate(raised, axis=0), both)
             parts = sums[:, :BLOCK] / sums[:, BLOCK:]
-            context[rows, columns] = jnp.where(first, parts[:BLOCK], parts[BLOCK:]).astype(BF16)
+            context[rows, columns] = jnp.where(first, parts[:pair], parts[pair:]).astype(BF16)
 
     loads[3].wait()
     ordered = jnp.concatenate([slots[index] for index in source], axis=0)

time: 62.9 us -> 62.8 us (level)
  no operation moved by 1% of the time
where the time goes in v5:
time: 62.8 us; the launch traced here: 62.7 us
  Pallas kernels  60.6 us (96%)
  local copies, waits for them, and re-layouts  2.06 us (3%)
    pallas_call x1, Pallas kernels, per_device(): pl.pallas_call(kernel, out_shape=jax.ShapeDtypeStruct((ROWS, WIDTH), BF16...  60.6 us
    unnamed x1, local copies, waits for them, and re-layouts  2.06 us

profile of v5, /device:TPU:1, one launch (start us, length us, event | category | flops | bytes accessed | tf_op | source)
XLA Modules:
  0.0 62.7 jit_solution(16692693220142800553)
XLA Ops:
  0.0 60.6 %shard_map.91 = bf16[512,768]{1,0:T(8,128)(2,1)} custom-call(bf16[4,128,768]{2,1,0:T(8,128)(2,1)} %bitcast.2, s32[4]{0:T(128)} %owner_ref.1, s32[1,512]{1,0:T(1,128)} %bitcast.3, s32[4,4]{1,0:T(4,128)} %mask_ref.1, bf16[768,2304]{1,0:T(8,128)(2,1)} %in_hbm.1, bf16[768,768]{1,0:T(8,128)(2,1)} %out_hbm.1, bf16[768,128]{1,0:T(8,128)(2,1)} %keys_hbm.1, ...), custom_call_target="tpu_custom_call" | custom-call | tf_op jit(solution)/shard_map/pallas_call | solution.py:336
  60.6 2.1 %copy.11 = bf16[512,768]{1,0:T(8,128)(2,1)} copy(bf16[512,768]{1,0:T(8,128)(2,1)} %shard_map.91) | data formatting | bytes 1572864
